TPU v7x, 32 devices: a whole 2x2x4 slice. The times are simulated.
32 devices in a mesh: groups: 2 (over y), seq: 4 (over z), dp: 2 (over x), tensor: 2 (over core).
Axes of the slice: x: 2, y: 2, z: 4, core: 2. Of those that a mesh axis runs over, the one named last changes fastest.
Arguments:
- queries: bfloat16 [4, 768, 1024], P(('groups', 'dp'), 'seq', 'tensor'), parts along dimension 0, may hold values from -80 to 80
- key_rows: bfloat16 [4, 768, 1024], P(('groups', 'dp'), 'seq', 'tensor'), parts along dimension 0, may hold values from -80 to 80
- value_rows: bfloat16 [4, 768, 1024], P(('groups', 'dp'), 'seq', 'tensor'), parts along dimension 0, may hold values from -6 to 6
- utterance: int32 [4, 768], P(('groups', 'dp'), 'seq'), parts along dimension 0, may hold values from 0 to 7, never falling along the last dimension, each value on 1 to 576 neighbouring positions
- cotangent: bfloat16 [4, 768, 1024], P(('groups', 'dp'), 'seq'), parts along dimension 0, may hold values from -6 to 6
- out_weight: bfloat16 [1024, 1024], P('tensor'), may hold values from -0.1875 to 0.1875
Outputs:
- grad_queries: bfloat16 [4, 768, 1024], P(('groups', 'dp'), 'seq', 'tensor'), parts along dimension 0
- grad_keys: bfloat16 [4, 768, 1024], P(('groups', 'dp'), 'seq', 'tensor'), parts along dimension 0
- grad_values: bfloat16 [4, 768, 1024], P(('groups', 'dp'), 'seq', 'tensor'), parts along dimension 0
- grad_out_weight: float32 [2048, 1024], P(('groups', 'tensor')), parts along dimension 0
There are 2 independent parts, one for each index of `groups`. A program takes and returns all parts, laid end to end along the dimension named above; an argument that names none is the same for every part. Nothing has to cross between parts.
Inputs may be any that keep to these rules, and one draw needn't show every extreme that they name: Within each packed sequence utterance numbers never fall, all 8 occur, each utterance spans 1 to 576 frames and one spans exactly 576.
All inputs are finite; a program needn't handle non-finite values.
Results may differ from a plain program's by a relative error of at most 0.02.
Values may be sent and summed in bfloat16 or wider, within the bound.
A program may use at most 128 MiB of HBM per device.

v0:
```python
import math
import jax
import jax.numpy as jnp
from jax import lax
from jax.sharding import PartitionSpec as P

HD = 64
MASKED_SCORE = -1e30


def heads_of(array):
    return array.reshape(array.shape[0], array.shape[1] // HD, HD)


def block_scores(query_block, key_block, query_utts, key_utts):
    scores = jnp.einsum(
        "qhd,khd->hqk", query_block, key_block, preferred_element_type=jnp.float32
    ) * HD ** (-0.5)
    same_utt = query_utts[:, None] == key_utts[None, :]
    return jnp.where(same_utt[None], scores, MASKED_SCORE)


def score_gradient(probs, dout_block, value_block, delta_rows):
    prob_grads = jnp.einsum(
        "qhd,khd->hqk", dout_block, value_block, preferred_element_type=jnp.float32
    )
    return (probs * (prob_grads - delta_rows[:, :, None]) * HD ** (-0.5)).astype(jnp.bfloat16)


def local(queries, key_rows, value_rows, utterance, cotangent, out_weight):
    own_queries = queries[0]
    frames_dev = own_queries.shape[0]
    width_dev = own_queries.shape[1]
    heads_dev = width_dev // HD
    query_heads = heads_of(own_queries)
    my_utts = utterance[0]
    utts_all = lax.all_gather(my_utts, "seq", axis=0, tiled=True)
    keys_all, values_all = (
        lax.all_gather(key_rows[0], "seq", axis=0, tiled=True),
        lax.all_gather(value_rows[0], "seq", axis=0, tiled=True),
    )
    frames_all = keys_all.shape[0]
    key_span = math.gcd(frames_all, 512)
    block_count = frames_all // key_span

    def key_block(block_index):
        offset = block_index * key_span
        key_block_rows = heads_of(lax.dynamic_slice_in_dim(keys_all, offset, key_span, 0))
        value_block_rows = heads_of(lax.dynamic_slice_in_dim(values_all, offset, key_span, 0))
        utt_block = lax.dynamic_slice_in_dim(utts_all, offset, key_span, 0)
        return (key_block_rows, value_block_rows, utt_block)

    def stats_step(block_index, carried):
        key_block_rows, value_block_rows, utt_block = key_block(block_index)
        running_max, running_sum = carried
        scores = block_scores(query_heads, key_block_rows, my_utts, utt_block)
        new_max = jnp.maximum(running_max, jnp.max(scores, axis=2))
        running_sum = running_sum * jnp.exp(running_max - new_max) + jnp.sum(
            jnp.exp(scores - new_max[:, :, None]), axis=2
        )
        return (new_max, running_sum)

    start_max = jnp.full((heads_dev, frames_dev), MASKED_SCORE, jnp.float32)
    start_sum = jnp.zeros((heads_dev, frames_dev), jnp.float32)
    running_max, running_sum = lax.fori_loop(0, block_count, stats_step, (start_max, start_sum))
    log_norm = running_max + jnp.log(running_sum)

    def output_step(block_index, carried):
        key_block_rows, value_block_rows, utt_block = key_block(block_index)
        scores = block_scores(query_heads, key_block_rows, my_utts, utt_block)
        probs_low = jnp.exp(scores - log_norm[:, :, None]).astype(jnp.bfloat16)
        return carried + jnp.einsum(
            "hqk,khd->hqd", probs_low, value_block_rows, preferred_element_type=jnp.float32
        )

    head_zeros = jnp.zeros((heads_dev, frames_dev, HD), jnp.float32)
    attended_acc = lax.fori_loop(0, block_count, output_step, head_zeros)
    attended = attended_acc.transpose(1, 0, 2).reshape(frames_dev, width_dev).astype(jnp.bfloat16)
    own_cot = cotangent[0]
    d_attended = lax.dot_general(
        own_cot, out_weight, (((1,), (1,)), ((), ())), preferred_element_type=jnp.float32
    ).astype(jnp.bfloat16)
    weight_term = lax.dot_general(
        attended, own_cot, (((0,), (0,)), ((), ())), preferred_element_type=jnp.float32
    )
    grad_weight = lax.psum(weight_term, ("seq", "dp"))
    dout_heads = heads_of(d_attended)
    row_delta = jnp.einsum(
        "qhd,qhd->hq", dout_heads.astype(jnp.float32), heads_of(attended).astype(jnp.float32)
    )

    def joint_step(block_index, carried):
        key_block_rows, value_block_rows, utt_block = key_block(block_index)
        query_acc_now, buffer = carried
        scores = block_scores(query_heads, key_block_rows, my_utts, utt_block)
        probs = jnp.exp(scores - log_norm[:, :, None])
        score_grads = score_gradient(probs, dout_heads, value_block_rows, row_delta)
        query_acc_now = query_acc_now + jnp.einsum(
            "hqk,khd->hqd", score_grads, key_block_rows, preferred_element_type=jnp.float32
        )
        key_part = jnp.einsum(
            "hqk,qhd->khd", score_grads, query_heads, preferred_element_type=jnp.float32
        )
        value_part = jnp.einsum(
            "hqk,qhd->khd",
            probs.astype(jnp.bfloat16),
            dout_heads,
            preferred_element_type=jnp.float32,
        )
        joined = jnp.concatenate(
            [key_part.reshape(key_span, width_dev), value_part.reshape(key_span, width_dev)], axis=1
        )
        buffer = lax.dynamic_update_slice_in_dim(buffer, joined, block_index * key_span, 0)
        return (query_acc_now, buffer)

    term_zeros = jnp.zeros((frames_all, 2 * width_dev), jnp.float32)
    query_acc, terms_all = lax.fori_loop(0, block_count, joint_step, (head_zeros, term_zeros))
    summed = lax.psum_scatter(terms_all, "seq", scatter_dimension=0, tiled=True)
    grad_key = summed[:, :width_dev].astype(jnp.bfloat16)
    grad_value = summed[:, width_dev:].astype(jnp.bfloat16)
    grad_query = query_acc.transpose(1, 0, 2).reshape(frames_dev, width_dev).astype(jnp.bfloat16)
    return (grad_query[None], grad_key[None], grad_value[None], grad_weight)


def solution(mesh):
    placed = (
        P(("groups", "dp"), "seq", "tensor"),
        P(("groups", "dp"), "seq", "tensor"),
        P(("groups", "dp"), "seq", "tensor"),
        P(("groups", "dp"), "seq"),
        P(("groups", "dp"), "seq", None),
        P("tensor", None),
    )
    return jax.shard_map(
        local,
        mesh=mesh,
        in_specs=placed,
        out_specs=(
            P(("groups", "dp"), "seq", "tensor"),
            P(("groups", "dp"), "seq", "tensor"),
            P(("groups", "dp"), "seq", "tensor"),
            P(("groups", "tensor"), None),
        ),
        check_vma=False,
    )
```

profile of v0, /device:TPU:0, one launch (start us, length us, event | category | flops | bytes accessed | tf_op | source)
XLA Modules:
  0.0 269.7 jit_solution(2575673276808037903)
XLA Ops:
  8.1 1.3 dynamic-slice
  11.0 9.9 %all-reduce = s32[768]{0:T(1024)S(1)} all-reduce(s32[768]{0:T(1024)S(1)} %dynamic-update-slice), channel_id=2, replica_groups=mesh['groups'=2,'seq'=4,'dp'=2,'tensor'=2] {'seq'}, use_global_device_ids=true, to_apply=%add | all-reduce | flops 768 | bytes 6144 | tf_op jit(solution)/shard_map/all_gather | solution.py:37
  20.9 18.1 %all-gather.1 = bf16[1,768,512]{2,1,0:T(8,128)(2,1)S(1)} all-gather(bf16[1,192,512]{2,1,0:T(8,128)(2,1)} %param.13), channel_id=3, replica_groups=mesh['groups'=2,'seq'=4,'dp'=2,'tensor'=2] {'seq'}, dimensions={1}, use_global_device_ids=true | all-gather | bytes 983040 | tf_op jit(solution)/shard_map/all_gather | solution.py:39
  40.3 7.3 %while.46 = (s32[]{:T(128)}, f32[8,192]{1,0:T(8,128)S(1)}, f32[8,192]{1,0:T(8,128)S(1)}, s32[1,192]{1,0:T(1,128)S(1)}, s32[768]{0:T(1024)S(1)}, /*index=5*/bf16[...) while((s32[]{:T(128)}, f32[8,192]{1,0:T(8,128)S(1)}, ...), condition=%wide.region_3.4_spmd.clone, body=%wide.region_0.3_spmd.clone.sunk | while | flops 52354564 | bytes 4310966 | solution.py:65
  47.6 17.9 %all-gather.2 = bf16[1,768,512]{2,1,0:T(8,128)(2,1)S(1)} all-gather(bf16[1,192,512]{2,1,0:T(8,128)(2,1)} %param.14), channel_id=4, replica_groups=mesh['groups'=2,'seq'=4,'dp'=2,'tensor'=2] {'seq'}, dimensions={1}, use_global_device_ids=true | all-gather | bytes 983040 | tf_op jit(solution)/shard_map/all_gather | solution.py:40
  68.0 6.3 %while.47 = (s32[]{:T(128)}, f32[8,192,64]{1,2,0:T(8,128)S(1)}, s32[1,192]{1,0:T(1,128)S(1)}, s32[768]{0:T(1024)S(1)}, bf16[768,512]{0,1:T(8,128)(2,1)}, /*index...) while((s32[]{:T(128)}, f32[8,192,64]{1,2,0:T(8,128)S(1)}, ...), condition=%wide.region_5.6_spmd.clone, body=%wide.region_4.5_spmd.clone.sunk | while | flops 102481928 | bytes 2664381 | solution.py:77
  74.3 1.7 fusion.18
  76.0 2.0 broadcast_in_dim.120.clone
  78.1 28.6 %while.48 = (s32[]{:T(128)}, f32[8,192,64]{1,2,0:T(8,128)}, f32[768,1024]{1,0:T(8,128)}, s32[1,192]{1,0:T(1,128)S(1)}, s32[768]{0:T(1024)S(1)}, /*index=5*/bf16[...) while((s32[]{:T(128)}, f32[8,192,64]{1,2,0:T(8,128)}, ...), condition=%wide.region_7.8_spmd.clone, body=%wide.region_6.7_spmd.clone.sunk | while | flops 255311872 | bytes 20561964 | solution.py:117
  80.0 1.4 fusion.81
  81.4 2.1 convolution_add_fusion.2
  83.5 1.2 fusion.82
  84.8 1.2 fusion.83
  89.4 1.4 fusion.81
  90.8 2.3 convolution_add_fusion.2
  93.1 1.2 fusion.82
  94.3 1.2 fusion.83
  99.0 1.4 fusion.81
  100.4 2.3 convolution_add_fusion.2
  103.9 1.2 fusion.83
  107.7 1.7 fusion.19
  111.4 69.4 %reduce-scatter.2.cloned.1.call-done = f32[192,1024]{1,0:T(8,128)} async-done(((f32[768,1024]{1,0:T(8,128)}), f32[192,1024]{1,0:T(8,128)}) %reduce-scatter.2.cloned.1.call-update) | async-done | bytes 786448 | tf_op jit(solution)/shard_map/reduce_scatter | solution.py:118
  182.7 76.3 %all-reduce.3.cloned.1.call-done = f32[512,1024]{1,0:T(8,128)} async-done(((f32[512,1024]{1,0:T(8,128)}), f32[512,1024]{1,0:T(8,128)}) %all-reduce.3.cloned.1.call-update) | async-done | bytes 2097168 | tf_op jit(solution)/shard_map/psum | solution.py:86
  259.1 3.2 %copy.74 = f32[512,1024]{1,0:T(8,128)} copy(f32[512,1024]{1,0:T(8,128)} %all-reduce.3.cloned.1.call-done) | data formatting | bytes 4194304
  (110 shorter events, 34.3 us)
Async XLA Ops:
  8.0 58.6 %copy-start = (bf16[512,1024]{1,0:T(8,128)(2,1)S(1)}, bf16[512,1024]{1,0:T(8,128)(2,1)}, u32[]{:S(2)}) copy-start(bf16[512,1024]{1,0:T(8,128)(2,1)} %param.17) | copy-start | bytes 3145732
  8.0 32.2 %copy-start.8 = (s32[1,192]{1,0:T(1,128)S(1)}, s32[1,192]{1,0:T(1,128)}, u32[]{:S(2)}) copy-start(s32[1,192]{1,0:T(1,128)} %param.15) | copy-start | bytes 2308
  8.0 32.1 %copy-start.9 = (bf16[1,192,512]{2,1,0:T(8,128)(2,1)S(1)}, bf16[1,192,512]{2,1,0:T(8,128)(2,1)}, u32[]{:S(2)}) copy-start(bf16[1,192,512]{2,1,0:T(8,128)(2,1)} %param.12) | copy-start | bytes 589828
  8.0 172.8 %reduce-scatter.2.cloned.1.call-start = ((), (), s32[]{:S(2)}) async-start(), calls=%async_computation.1 | async-start | bytes 3932160 | tf_op jit(solution)/shard_map/reduce_scatter | solution.py:118
  47.6 19.0 %copy-start.5 = (bf16[1,192,1024]{2,1,0:T(8,128)(2,1)S(1)}, bf16[1,192,1024]{2,1,0:T(8,128)(2,1)}, u32[]{:S(2)}) copy-start(bf16[1,192,1024]{2,1,0:T(8,128)(2,1)} %param.16) | copy-start | bytes 1179652
  78.1 1.9 copy-start.1
  79.2 0.8 copy-start.3
  86.4 1.1 copy-start.2
  87.4 1.9 copy-start.1
  88.6 0.8 copy-start.3
  95.9 1.1 copy-start.2
  97.1 1.9 copy-start.1
  98.2 0.8 copy-start.3
  105.6 1.1 copy-start.2
  106.7 1.0 copy-start.6
  106.7 1.1 copy-start.7
  106.7 152.4 %all-reduce.3.cloned.1.call-start = ((), (), s32[]{:S(2)}) async-start(), calls=%async_computation.2 | async-start | bytes 4194304 | tf_op jit(solution)/shard_map/psum | solution.py:86
  109.5 1.0 copy-start.4
Sparse Core Ops, SparseCore 0:
  106.8 73.9 reduce-scatter.1
Sparse Core Ops, SparseCore 1:
  111.4 147.7 all-reduce.2
where the time goes:
time: 271 us; the launch traced here: 270 us
  waiting for transfers between devices  146 us (54%)
  blocking collectives  45.8 us (17%)
  local copies, waits for them, and re-layouts  28.9 us (11%)
  matrix products  26.4 us (10%)
  between operations  16.3 us (6%)
  other arithmetic  5.89 us (2%)
    psum x1, waiting for transfers between devices, local(): grad_weight = lax.psum(weight_term, ('seq', 'dp'))  76.3 us
    reduce_scatter x1, waiting for transfers between devices, local(): summed = lax.psum_scatter(terms_all, 'seq', scatter_dimension=0, tiled=True)  69.4 us
    all_gather x1, blocking collectives, local(): lax.all_gather(key_rows[0], 'seq', axis=0, tiled=True)  18.1 us
    all_gather x1, blocking collectives, local(): lax.all_gather(value_rows[0], 'seq', axis=0, tiled=True)  17.9 us
    unnamed x22, local copies, waits for them, and re-layouts  10.6 us
    all_gather x1, blocking collectives, local(): utts_all = lax.all_gather(my_utts, 'seq', axis=0, tiled=True)  9.89 us
    dot_general x3, matrix products, joint_step(): jnp.einsum('hqk,khd->hqd', score_grads, key_block_rows, preferred_element...  6.76 us
    dynamic_slice x6, local copies, waits for them, and re-layouts, key_block(): lax.dynamic_slice_in_dim(values_all, offset, key_span, 0)  6.7 us
  transfers between devices with their start and end apart: 2, of which 2 were waited for; matrix products, arithmetic and copies ran while one was open for 2% of the time, Pallas kernels for 0%

commit v1 on v0

--- a/solution.py
+++ b/solution.py
@@ -83,7 +83,7 @@
     weight_term = lax.dot_general(
         attended, own_cot, (((0,), (0,)), ((), ())), preferred_element_type=jnp.float32
     )
-    grad_weight = lax.psum(weight_term, ("seq", "dp"))
+    grad_weight = jnp.sum(lax.all_gather(weight_term, ("seq", "dp")), axis=0)
     dout_heads = heads_of(d_attended)
     row_delta = jnp.einsum(
         "qhd,qhd->hq", dout_heads.astype(jnp.float32), heads_of(attended).astype(jnp.float32)

time: 271 us -> 392 us (1.45)
  waiting for transfers between devices: 146 us -> 267 us
  other arithmetic: 5.89 us -> 17.1 us
  matrix products: 26.4 us -> 17.8 us
    all_gather x0 -> x1, waiting for transfers between devices: none -> 166 us  [local(): grad_weight = jnp.sum(lax.all_gather(weight_term, ('seq', 'dp')), axis=0)]
    psum x1 -> x0, waiting for transfers between devices: 76.3 us -> none  [local(): grad_weight = lax.psum(weight_term, ('seq', 'dp'))]
    reduce_scatter x1, waiting for transfers between devices: 69.4 us -> 101 us  [local(): summed = lax.psum_scatter(terms_all, 'seq', scatter_dimension=0, tiled=True)]
    reduce_sum x0 -> x1, other arithmetic: none -> 9.28 us  [local(): grad_weight = jnp.sum(lax.all_gather(weight_term, ('seq', 'dp')), axis=0)]
    unnamed x22 -> x23, local copies, waits for them, and re-layouts: 10.6 us -> 6.15 us
  transfers between devices with their start and end apart: 2 -> 2, of which waited for: 2 -> 2; matrix products, arithmetic and copies ran while one was open for 2% -> 1% of each run, Pallas kernels for 0% -> 0%
where the time goes in v1:
time: 392 us
  waiting for transfers between devices  267 us (68%)
  blocking collectives  45.5 us (12%)
  local copies, waits for them, and re-layouts  27.1 us (7%)
  matrix products  17.8 us (5%)
  other arithmetic  17.1 us (4%)
  between operations  16.3 us (4%)
    all_gather x1, waiting for transfers between devices, local(): grad_weight = jnp.sum(lax.all_gather(weight_term, ('seq', 'dp')), axis=0)  166 us
    reduce_scatter x1, waiting for transfers between devices, local(): summed = lax.psum_scatter(terms_all, 'seq', scatter_dimension=0, tiled=True)  101 us
    all_gather x1, blocking collectives, local(): lax.all_gather(key_rows[0], 'seq', axis=0, tiled=True)  21.6 us
    all_gather x1, blocking collectives, local(): lax.all_gather(value_rows[0], 'seq', axis=0, tiled=True)  17.1 us
    reduce_sum x1, other arithmetic, local(): grad_weight = jnp.sum(lax.all_gather(weight_term, ('seq', 'dp')), axis=0)  9.28 us
    dynamic_update_slice x6, local copies, waits for them, and re-layouts, joint_step(): lax.dynamic_update_slice_in_dim(buffer, joined, block_index * key_span, 0)  7.89 us
  transfers between devices with their start and end apart: 2, of which 2 were waited for; matrix products, arithmetic and copies ran while one was open for 1% of the time, Pallas kernels for 0%

profile of v1, /device:TPU:0, one launch (start us, length us, event | category | flops | bytes accessed | tf_op | source)
XLA Modules:
  0.0 391.6 jit_solution(9558299042671618196)
XLA Ops:
  8.1 21.6 %all-gather.1 = bf16[1,768,512]{2,1,0:T(8,128)(2,1)S(1)} all-gather(bf16[1,192,512]{2,1,0:T(8,128)(2,1)} %param.13), channel_id=3, replica_groups=mesh['groups'=2,'seq'=4,'dp'=2,'tensor'=2] {'seq'}, dimensions={1}, use_global_device_ids=true | all-gather | bytes 983040 | tf_op jit(solution)/shard_map/all_gather | solution.py:39
  29.8 1.2 copy.30
  32.6 6.7 %all-reduce = s32[768]{0:T(1024)S(1)} all-reduce(s32[768]{0:T(1024)S(1)} %dynamic-update-slice), channel_id=2, replica_groups=mesh['groups'=2,'seq'=4,'dp'=2,'tensor'=2] {'seq'}, use_global_device_ids=true, to_apply=%add | all-reduce | flops 768 | bytes 6144 | tf_op jit(solution)/shard_map/all_gather | solution.py:37
  39.3 7.3 %while.46 = (s32[]{:T(128)}, f32[8,192]{1,0:T(8,128)S(1)}, f32[8,192]{1,0:T(8,128)S(1)}, s32[1,192]{1,0:T(1,128)S(1)}, s32[768]{0:T(1024)S(1)}, /*index=5*/bf16[...) while((s32[]{:T(128)}, f32[8,192]{1,0:T(8,128)S(1)}, ...), condition=%wide.region_3.4_spmd.clone, body=%wide.region_0.3_spmd.clone.sunk | while | flops 52354564 | bytes 4310958 | solution.py:65
  46.6 17.1 %all-gather.2 = bf16[1,768,512]{2,1,0:T(8,128)(2,1)S(1)} all-gather(bf16[1,192,512]{2,1,0:T(8,128)(2,1)} %param.14), channel_id=4, replica_groups=mesh['groups'=2,'seq'=4,'dp'=2,'tensor'=2] {'seq'}, dimensions={1}, use_global_device_ids=true | all-gather | bytes 983040 | tf_op jit(solution)/shard_map/all_gather | solution.py:40
  63.7 1.2 copy.31
  64.9 6.4 %while.47 = (s32[]{:T(128)}, f32[8,192,64]{1,2,0:T(8,128)S(1)}, s32[1,192]{1,0:T(1,128)S(1)}, s32[768]{0:T(1024)S(1)}, bf16[768,512]{0,1:T(8,128)(2,1)}, /*index...) while((s32[]{:T(128)}, f32[8,192,64]{1,2,0:T(8,128)S(1)}, ...), condition=%wide.region_5.6_spmd.clone, body=%wide.region_4.5_spmd.clone.sunk | while | flops 102481928 | bytes 2664373 | solution.py:77
  64.9 1.1 constant_dynamic-slice_fusion.9
  67.1 1.1 constant_dynamic-slice_fusion.9
  69.2 1.1 constant_dynamic-slice_fusion.9
  72.7 2.0 broadcast_in_dim.120.clone
  74.8 26.2 %while.48 = (s32[]{:T(128)}, f32[8,192,64]{1,2,0:T(8,128)}, f32[768,1024]{1,0:T(8,128)}, s32[1,192]{1,0:T(1,128)S(1)}, s32[768]{0:T(1024)S(1)}, /*index=5*/bf16[...) while((s32[]{:T(128)}, f32[8,192,64]{1,2,0:T(8,128)}, ...), condition=%wide.region_7.8_spmd.clone, body=%wide.region_6.7_spmd.clone.sunk | while | flops 255311872 | bytes 18989036 | solution.py:117
  78.6 1.6 copy.47
  81.3 2.1 convolution_add_fusion.2
  87.2 1.6 copy.47
  88.8 1.1 constant_dynamic-update-slice_fusion.2
  89.9 2.3 convolution_add_fusion.2
  96.1 1.6 copy.47
  98.7 2.3 convolution_add_fusion.2
  102.0 1.7 fusion.19
  105.7 101.1 %reduce-scatter.2.cloned.1.call-done = f32[192,1024]{1,0:T(8,128)} async-done(((f32[768,1024]{1,0:T(8,128)}), f32[192,1024]{1,0:T(8,128)}) %reduce-scatter.2.cloned.1.call-update) | async-done | bytes 786448 | tf_op jit(solution)/shard_map/reduce_scatter | solution.py:118
  206.8 1.2 convert.4
  208.7 166.2 %all-gather.6.cloned.1.call-done = f32[4096,1024]{1,0:T(8,128)} async-done(((f32[512,1024]{1,0:T(8,128)}), f32[4096,1024]{1,0:T(8,128)}) %all-gather.6.cloned.1.call-update) | async-done | bytes 16777232 | tf_op jit(solution)/shard_map/all_gather | solution.py:86
  374.9 9.3 %reduce_sum.22 = f32[512,1024]{1,0:T(8,128)} reduce(f32[8,512,1024]{2,1,0:T(8,128)} %bitcast.147, f32[]{:T(128)} %constant.139.clone.1), dimensions={0}, to_apply=%region_9.10 | reduce | flops 3670016 | bytes 18874372 | tf_op jit(solution)/shard_map/reduce_sum | solution.py:86
  (100 shorter events, 29.8 us)
Async XLA Ops:
  8.0 63.3 %copy-start = (bf16[512,1024]{1,0:T(8,128)(2,1)S(1)}, bf16[512,1024]{1,0:T(8,128)(2,1)}, u32[]{:S(2)}) copy-start(bf16[512,1024]{1,0:T(8,128)(2,1)} %param.17) | copy-start | bytes 3145732
  8.0 23.1 %copy-start.8 = (u32[32]{0:T(128)S(1)}, u32[32]{0:T(128)}, u32[]{:S(2)}) copy-start(u32[32]{0:T(128)} %constant.148) | copy-start | bytes 388
  8.0 22.9 %copy-start.7 = (bf16[1,192,512]{2,1,0:T(8,128)(2,1)S(1)}, bf16[1,192,512]{2,1,0:T(8,128)(2,1)}, u32[]{:S(2)}) copy-start(bf16[1,192,512]{2,1,0:T(8,128)(2,1)} %param.12) | copy-start | bytes 589828
  8.0 24.3 %copy-start.6 = (s32[1,192]{1,0:T(1,128)S(1)}, s32[1,192]{1,0:T(1,128)}, u32[]{:S(2)}) copy-start(s32[1,192]{1,0:T(1,128)} %param.15) | copy-start | bytes 2308
  8.0 198.7 %reduce-scatter.2.cloned.1.call-start = ((), (), s32[]{:S(2)}) async-start(), calls=%async_computation.1 | async-start | bytes 3932160 | tf_op jit(solution)/shard_map/reduce_scatter | solution.py:118
  64.9 6.4 %copy-start.3 = (bf16[1,192,1024]{2,1,0:T(8,128)(2,1)S(1)}, bf16[1,192,1024]{2,1,0:T(8,128)(2,1)}, u32[]{:S(2)}) copy-start(bf16[1,192,1024]{2,1,0:T(8,128)(2,1)} %param.16) | copy-start | bytes 1179652
  75.8 0.8 copy-start.1
  84.4 0.8 copy-start.1
  93.3 0.8 copy-start.1
  101.0 1.0 copy-start.4
  101.0 1.1 copy-start.5
  101.0 273.9 %all-gather.6.cloned.1.call-start = ((), (), s32[]{:S(2)}) async-start(), calls=%async_computation.2 | async-start | bytes 18874368 | tf_op jit(solution)/shard_map/all_gather | solution.py:86
  103.8 1.0 copy-start.2
Sparse Core Ops, SparseCore 0:
  101.1 105.6 reduce-scatter.1
Sparse Core Ops, SparseCore 1:
  104.2 270.6 all-gather.5
